TPU v7x, 32 devices: a whole 2x2x4 slice. The times are simulated.
32 devices in a mesh: ctx: 16 (over z, y, x), ch: 2 (over core).
Axes of the slice: x: 2, y: 2, z: 4, core: 2. Of those that a mesh axis runs over, the one named last changes fastest.
Arguments:
- value_in: bfloat16 [2048, 4096], P('ctx', 'ch'), may hold values from -6 to 6
- key_in: bfloat16 [2048, 4096], P('ctx', 'ch'), may hold values from -6 to 6
- gate_short: bfloat16 [2048, 4096], P('ctx', 'ch'), may hold values from -6 to 6
- gate_long: bfloat16 [2048, 4096], P('ctx', 'ch'), may hold values from -6 to 6
- short_filter: bfloat16 [256, 128], P('ch'), may hold values from -0.5 to 0.5
- long_filter: float32 [4096, 2048], P(('ch', 'ctx')), may hold values from -2 to 2
- skip_gain: float32 [4096], P('ch'), may hold values from 0.5 to 1.5
- out_weight: bfloat16 [4096, 4096], P('ctx', 'ch'), may hold values from -0.09375 to 0.09375
Outputs:
- layer_out: bfloat16 [2048, 4096], P('ctx', 'ch')
All inputs are finite; a program needn't handle non-finite values.
Results may differ from a plain program's by a relative error of at most 0.0067.
Values may be sent and summed in bfloat16 or wider, within the bound.
A program may use at most 64 MiB of HBM per device.

v0:
```python
import math

import jax
import jax.numpy as jnp
from jax import lax
from jax.sharding import PartitionSpec as P


def passed_along(value, axis, steps):
    count = lax.axis_size(axis)
    first, last = (max(0, -steps), min(count, count - steps))
    return lax.ppermute(value, axis, [(source, source + steps) for source in range(first, last)])


def toeplitz(tap_rows, width):
    group_count, tap_count = tap_rows.shape
    band_width = width + tap_count - 1
    band_line = jnp.concatenate(
        [
            jnp.zeros((group_count, width), tap_rows.dtype),
            tap_rows[:, ::-1],
            jnp.zeros((group_count, width), tap_rows.dtype),
        ],
        1,
    )
    line_len = band_line.shape[1]
    row_span = line_len - 1
    tiled = jnp.tile(band_line, (1, width))[:, : width * row_span].reshape(
        group_count, width, row_span
    )
    return tiled[:, :, width : width + band_width]


def short_blocks(padded, tap_rows, width):
    group_count, group_width, extended = padded.shape
    tap_count = tap_rows.shape[1]
    seq_len = extended - (tap_count - 1)
    block_count = seq_len // width
    inner_rows = padded[:, :, tap_count - 1 :].reshape(group_count, group_width, block_count, width)
    earlier = padded[:, :, :seq_len].reshape(group_count, group_width, block_count, width)[
        :, :, :, : tap_count - 1
    ]
    windows = jnp.concatenate([earlier, inner_rows], -1)
    band = toeplitz(tap_rows, width)
    result = jnp.einsum("gte,gcbe->gcbt", band, windows, preferred_element_type=jnp.float32)
    return result.reshape(group_count, group_width, seq_len)


def tables(size):
    counter = jnp.arange(size, dtype=jnp.int32)
    angle = 2.0 * math.pi / size * (counter[:, None] * counter[None, :] % size).astype(jnp.float32)
    return (jnp.cos(angle), jnp.sin(angle))


def left_mul(matrix, signal):
    return jnp.einsum("kn,cnq->ckq", matrix, signal, precision=lax.Precision.HIGHEST)


def right_mul(signal, matrix):
    return jnp.einsum("ckn,nq->ckq", signal, matrix, precision=lax.Precision.HIGHEST)


def long_conv(local_rows, long_filter):
    rows, seq_len = local_rows.shape
    span_len = 2 * seq_len
    second_len = min(2 ** ((span_len.bit_length() - 1) // 2), span_len & -span_len)
    first_len = span_len // second_len
    cos_p, sin_p = tables(first_len)
    cos_q, sin_q = tables(second_len)
    first_idx = jnp.arange(first_len, dtype=jnp.int32)
    second_idx = jnp.arange(second_len, dtype=jnp.int32)
    twist_angle = (
        2.0
        * math.pi
        / span_len
        * (first_idx[:, None] * second_idx[None, :] % span_len).astype(jnp.float32)
    )
    twist_re = jnp.cos(twist_angle)
    twist_im = jnp.sin(twist_angle)

    def spectrum(signal):
        shaped = jnp.concatenate([signal, jnp.zeros_like(signal)], 1).reshape(
            rows, first_len, second_len
        )
        section_re = left_mul(cos_p, shaped)
        section_im = -left_mul(sin_p, shaped)
        turned_re = section_re * twist_re + section_im * twist_im
        turned_im = section_im * twist_re - section_re * twist_im
        final_re = right_mul(turned_re, cos_q) + right_mul(turned_im, sin_q)
        final_im = right_mul(turned_im, cos_q) - right_mul(turned_re, sin_q)
        return (final_re, final_im)

    data_re, data_im = spectrum(local_rows.astype(jnp.float32))
    filt_re, filt_im = spectrum(long_filter)
    prod_re = data_re * filt_re - data_im * filt_im
    prod_im = data_re * filt_im + data_im * filt_re
    back_re = right_mul(prod_re, cos_q) - right_mul(prod_im, sin_q)
    back_im = right_mul(prod_im, cos_q) + right_mul(prod_re, sin_q)
    untwist_re = back_re * twist_re - back_im * twist_im
    untwist_im = back_re * twist_im + back_im * twist_re
    signal_out = (left_mul(cos_p, untwist_re) - left_mul(sin_p, untwist_im)) / span_len
    return signal_out.reshape(rows, span_len)[:, :seq_len].astype(jnp.bfloat16)


def shards(
    value_in, key_in, gate_short, gate_long, short_filter, long_filter, skip_gain, out_weight
):
    tok_rows, channels = value_in.shape
    ctx_ways = lax.axis_size("ctx")
    per_dev = channels // ctx_ways
    seq_len = tok_rows * ctx_ways
    tap_count = short_filter.shape[1]
    group_size = channels // short_filter.shape[0]
    product = (value_in.astype(jnp.float32) * key_in.astype(jnp.float32)).astype(jnp.bfloat16).T
    gate_rows = gate_short.T
    prior_rim = passed_along(product, "ctx", 1)
    extended = jnp.concatenate([prior_rim[:, 1:], product], 1)
    short_out = short_blocks(
        extended.reshape(channels // group_size, group_size, tok_rows + tap_count - 1),
        short_filter,
        min(512, tok_rows),
    ).reshape(channels, tok_rows)
    mid_rows = (gate_rows.astype(jnp.float32) * short_out).astype(jnp.bfloat16)
    regrouped = lax.all_to_all(
        mid_rows.reshape(ctx_ways, per_dev, tok_rows),
        "ctx",
        split_axis=0,
        concat_axis=2,
        tiled=True,
    )
    long_part = long_conv(regrouped.reshape(per_dev, seq_len), long_filter)
    returned = lax.all_to_all(
        long_part.reshape(1, per_dev, seq_len), "ctx", split_axis=2, concat_axis=0, tiled=True
    )
    long_rows = returned.reshape(channels, tok_rows)
    gated_rows = (
        gate_long.T.astype(jnp.float32)
        * (long_rows.astype(jnp.float32) + skip_gain[:, None] * mid_rows.astype(jnp.float32))
    ).astype(jnp.bfloat16)
    features = lax.all_gather(gated_rows, "ch", axis=0, tiled=True)
    projected = lax.dot_general(
        features,
        lax.all_gather(out_weight, "ctx", axis=0, tiled=True),
        (((0,), (0,)), ((), ())),
        preferred_element_type=jnp.float32,
    )
    return projected.astype(jnp.bfloat16)


def solution(mesh):
    in_specs = (
        P("ctx", "ch"),
        P("ctx", "ch"),
        P("ctx", "ch"),
        P("ctx", "ch"),
        P("ch", None),
        P(("ch", "ctx"), None),
        P("ch"),
        P("ctx", "ch"),
    )
    out_specs = P("ctx", "ch")
    return jax.shard_map(shards, mesh=mesh, in_specs=in_specs, out_specs=out_specs, check_vma=False)
```

profile of v0, /device:TPU:0, one launch (start us, length us, event | category | flops | bytes accessed | tf_op | source)
XLA Modules:
  0.0 425.6 jit_solution(6061498678841540570)
XLA Ops:
  6.5 1.3 fusion.64
  7.9 4.9 %collective-permute-start = (bf16[2048,128]{0,1:T(8,128)(2,1)S(1)}, bf16[2048,128]{0,1:T(8,128)(2,1)S(1)}, u32[]{:S(2)}, u32[]{:S(2)}) collective-permute-start(bf16[2048,128]{0,1:T(8,128)(2,1)S(1)} %fusion.64), channel_id=1, source_target_pairs={{0,2},{2,4},{4,6},{6,8},{8,10},{10,12},{12,14},{14,16},{16,18},{18... | collective-permute-start | bytes 1572872 | tf_op jit(solution)/shard_map/ppermute | solution.py:12
  12.7 0.8 rev.3
  13.6 5.6 %tile.4 = bf16[128,128,384]{2,1,0:T(8,128)(2,1)} broadcast(bf16[128,384]{1,0:T(8,128)(2,1)S(1)} %pad_maximum_fusion.1), dimensions={0,2} | broadcast | bytes 12681216 | tf_op jit(solution)/shard_map/tile | solution.py:28
  19.2 12.5 %copy.171 = bf16[16,8,128,384]{3,1,2,0:T(8,128)(2,1)S(1)} copy(bf16[16,8,128,384]{3,2,1,0:T(8,128)(2,1)} %bitcast.135) | data formatting | bytes 25165824
  31.7 5.1 %slice.33 = bf16[128,49024]{1,0:T(8,128)(2,1)} slice(bf16[128,49152]{1,0:T(8,128)(2,1)S(1)} %bitcast.136), slice={[0:128], [0:49024]} | slice | bytes 25100288 | tf_op jit(solution)/shard_map/slice | solution.py:28
  36.9 30.9 %reshape.93 = bf16[128,128,383]{2,1,0:T(8,128)(2,1)} reshape(bf16[128,49024]{1,0:T(8,128)(2,1)} %slice.33) | data formatting | bytes 25100288 | tf_op jit(solution)/shard_map/reshape | solution.py:28
  67.8 0.3 copy.109
  68.4 0.5 copy.110
  69.2 5.7 %fusion = f32[128,16,128]{2,1,0:T(8,128)S(1)} fusion(bf16[128,128,383]{2,1,0:T(8,128)(2,1)} %reshape.93, bf16[128,16,1,128]{3,1,0,2:T(8,128)(2,1)S(1)} %get-tuple-element.12, bf16[128,16,1,127]{3,1,0,2:T(8,128)(2,1)S(1)} %bitcast.146), kind=kOutput, calls=%fused_computation | convolution fusion | flops 135782400 | bytes 10481664 | tf_op jit(solution)/shard_map/gte,gcbe->gcbt/dot_general | solution.py:45
  74.8 0.9 fusion.55
  75.8 6.4 %all-to-all-start = ((bf16[16,128,128]{2,1,0:T(8,128)(2,1)}), bf16[16,128,128]{2,1,0:T(8,128)(2,1)}, u32[]{:S(2)}, u32[]{:S(2)}) async-start(bf16[16,128,128]{2,1,0:T(8,128)(2,1)} %bitcast.8), calls=%async_computation | async-start | bytes 1048576 | tf_op jit(solution)/shard_map/all_to_all | solution.py:124
  82.7 0.3 copy.120
  83.1 4.6 %fusion.22 = f32[128,64,64]{0,2,1:T(8,128)} fusion(f32[128,64,64]{0,2,1:T(8,128)S(1)} %bitcast.137), kind=kOutput, calls=%fused_computation.36 | convolution fusion | flops 402710528 | bytes 4194304 | tf_op jit(solution)/shard_map/kn,cnq->ckq/dot_general | solution.py:56
  87.8 8.9 %all-to-all-done = bf16[16,128,128]{2,1,0:T(8,128)(2,1)} async-done(((bf16[16,128,128]{2,1,0:T(8,128)(2,1)}), bf16[16,128,128]{2,1,0:T(8,128)(2,1)}, u32[]{:S(2)}, u32[]{:S(2)}) %all-to-all-start) | async-done | bytes 524320 | tf_op jit(solution)/shard_map/all_to_all | solution.py:124
  96.6 1.3 copy.111
  98.1 1.5 fusion.60
  99.6 1.5 fusion.62
  101.2 4.4 %fusion.2 = (f32[128,64,64]{0,1,2:T(8,128)S(1)}, f32[128,64,64]{0,1,2:T(8,128)S(1)}, f32[128,64,64]{0,1,2:T(8,128)S(1)}, f32[128,64,64]{0,1,2:T(8,128)S(1)}) fusion(f32[128,64,64]{0,2,1:T(8,128)S(1)} %copy-done, f32[64,64]{0,1:T(8,128)S(1)} %copy.115, f32[64,64]{0,1:T(8,128)S(1)} %copy.113, f32[128,64,64]{0,2,1:T(8,128)S(1)} %fusion.62, ...), kind=kOutput, calls=%fused_computation.5 | convolution fusion | flops 410050560 | bytes 16809984 | tf_op jit(solution)/shard_map/kn,cnq->ckq/dot_general | solution.py:56
  105.6 3.6 fusion.16
  109.2 3.4 fusion.14
  112.6 3.4 fusion.28
  116.0 3.6 fusion.26
  119.6 3.4 fusion.40
  123.0 3.4 fusion.43
  126.4 3.4 fusion.34
  129.9 4.6 %multiply_subtract_fusion = (f32[128,64,64]{0,2,1:T(8,128)S(1)}, f32[128,64,64]{0,2,1:T(8,128)S(1)}) fusion(f32[128,64,64]{0,2,1:T(8,128)S(1)} %fusion.43, f32[128,64,64]{0,2,1:T(8,128)S(1)} %fusion.34, f32[128,64,64]{0,2,1:T(8,128)S(1)} %fusion.40, f32[128,64,64]{0,2,1:T(8,128)S(1)} %fusion.26, f32[128,64,64]{0,1,2:T(8,128)S(1)} %get-tuple-element.14), kind=kOutput, calls=%fused_computation.27 | convolution fusion | flops 406380544 | bytes 14680064 | tf_op jit(solution)/shard_map/ckn,nq->ckq/dot_general | solution.py:60
  134.5 2.1 fusion.71
  136.6 2.1 fusion.80
  138.7 2.1 fusion.69
  140.8 2.1 fusion.82
  142.9 8.6 %fusion.6 = f32[128,64,64]{0,2,1:T(8,128)S(1)} fusion(f32[64,64]{0,1:T(8,128)S(1)} %copy.115, f32[64,64]{0,1:T(8,128)S(1)} %copy.113, f32[128,64,64]{0,2,1:T(8,128)S(1)} %fusion.71, f32[128,64,64]{0,2,1:T(8,128)S(1)} %fusion.82, f32[128,64,64]{0,2,1:T(8,128)S(1)} %fusion.69, f32[128,64,64]{0,2,1:T(8,128)S(1)} %fusion.80), kind=kOutput, calls=%fused_computation.18 | convolution fusion | flops 405331968 | bytes 10518528 | tf_op jit(solution)/shard_map/kn,cnq->ckq/dot_general | solution.py:56
  151.5 10.7 %fusion.48 = bf16[128,64,64]{0,1,2:T(8,128)(2,1)S(1)} fusion(f32[128,64,64]{0,2,1:T(8,128)S(1)} %fusion.6, f32[64,64]{0,1:T(8,128)S(1)} %copy.115, f32[64,64]{0,1:T(8,128)S(1)} %copy.113, f32[128,64,64]{0,2,1:T(8,128)S(1)} %fusion.71, f32[128,64,64]{0,2,1:T(8,128)S(1)} %fusion.82, f32[128,64,64]{0,2,1:T(8,128)S(1)} %fusion.69, f32[128,64,64]{0,2,1:T(8,128)S(1)} %fusion.80), kind=kOutput, calls=%fused_computation.52 | convolution fusion | flops 406904832 | bytes 11567104 | tf_op jit(solution)/shard_map/kn,cnq->ckq/dot_general | solution.py:56
  162.2 0.7 copy.143
  162.9 8.1 %copy.237 = bf16[1,128,2048]{1,0,2:T(2,128)(2,1)S(1)} copy(bf16[1,128,2048]{1,2,0:T(8,128)(2,1)S(1)} %slice_bitcast_fusion) | data formatting | bytes 1048576 | tf_op jit(solution)/shard_map/reshape | solution.py:133
  171.1 0.5 broadcast.212
  171.6 11.8 %reduce = bf16[2048,128]{1,0:T(8,128)(2,1)S(1)} reduce(bf16[2048,1,128]{2,1,0:T(2,128)(2,1)S(1)} %bitcast.143, bf16[]{:T(256)} %broadcast.212), dimensions={1}, to_apply=%bitcast.133.reduce_sub_computation | reduce | bytes 1048578
  183.4 0.9 reshape.116
  184.3 3.9 all-to-all-start.1
  188.3 0.3 copy.108
  188.6 14.1 %all-to-all-done.1 = bf16[16,2,8192]{2,1,0:T(2,128)(2,1)S(1)} async-done(((bf16[16,2,8192]{2,1,0:T(2,128)(2,1)}), bf16[16,2,8192]{2,1,0:T(2,128)(2,1)S(1)}, u32[]{:S(2)}, u32[]{:S(2)}) %all-to-all-start.1) | async-done | bytes 524320 | tf_op jit(solution)/shard_map/all_to_all | solution.py:132
  202.6 0.5 reshape.117
  203.4 0.3 copy.146
  204.0 2.3 fusion.54
  206.3 0.7 all-gather.5.cloned.1.call-update
  207.0 6.7 %all-gather.3.cloned.1.call-done = bf16[4096,128]{1,0:T(8,128)(2,1)} async-done(((bf16[2048,128]{1,0:T(8,128)(2,1)}), bf16[4096,128]{1,0:T(8,128)(2,1)}) %all-gather.3.cloned.1.call-update) | async-done | bytes 1048592 | tf_op jit(solution)/shard_map/all_gather | solution.py:140
  213.7 195.6 %all-gather.5.cloned.1.call-done = bf16[4096,2048]{1,0:T(8,128)(2,1)} async-done(((bf16[256,2048]{1,0:T(8,128)(2,1)}), bf16[4096,2048]{1,0:T(8,128)(2,1)}) %all-gather.5.cloned.1.call-update) | async-done | bytes 16777232 | tf_op jit(solution)/shard_map/all_gather | solution.py:143
  409.3 9.3 %convolution_convert_fusion = bf16[128,2048]{1,0:T(8,128)(2,1)} fusion(bf16[4096,128]{1,0:T(8,128)(2,1)} %all-gather.3.cloned.1.call-done, bf16[4096,2048]{1,0:T(8,128)(2,1)} %all-gather.5.cloned.1.call-done), kind=kOutput, calls=%fused_computation.2 | convolution fusion | flops 2147745792 | bytes 18350080 | tf_op jit(solution)/shard_map/dot_general | solution.py:141
  (28 shorter events, 1.9 us)
Async XLA Ops:
  7.9 60.2 %collective-permute-start = (bf16[2048,128]{0,1:T(8,128)(2,1)S(1)}, bf16[2048,128]{0,1:T(8,128)(2,1)S(1)}, u32[]{:S(2)}, u32[]{:S(2)}) collective-permute-start(bf16[2048,128]{0,1:T(8,128)(2,1)S(1)} %fusion.64), channel_id=1, source_target_pairs={{0,2},{2,4},{4,6},{6,8},{8,10},{10,12},{12,14},{14,16},{16,18},{18... | collective-permute-start | bytes 1572872 | tf_op jit(solution)/shard_map/ppermute | solution.py:12
  36.9 30.9 %copy-start.2 = (bf16[128,2048]{1,0:T(8,128)(2,1)S(1)}, bf16[128,2048]{1,0:T(8,128)(2,1)}, u32[]{:S(2)}) copy-start(bf16[128,2048]{1,0:T(8,128)(2,1)} %param.10) | copy-start | bytes 1572868
  74.8 7.8 %copy-start.1 = (f32[128,2048]{1,0:T(8,128)S(1)}, f32[128,2048]{1,0:T(8,128)}, u32[]{:S(2)}) copy-start(f32[128,2048]{1,0:T(8,128)} %param.13) | copy-start | bytes 3145732
  75.8 20.9 %all-to-all-start = ((bf16[16,128,128]{2,1,0:T(8,128)(2,1)}), bf16[16,128,128]{2,1,0:T(8,128)(2,1)}, u32[]{:S(2)}, u32[]{:S(2)}) async-start(bf16[16,128,128]{2,1,0:T(8,128)(2,1)} %bitcast.8), calls=%async_computation | async-start | bytes 1048576 | tf_op jit(solution)/shard_map/all_to_all | solution.py:124
  99.6 1.6 copy-start
  171.1 17.2 %copy-start.3 = (bf16[128,2048]{1,0:T(8,128)(2,1)S(1)}, bf16[128,2048]{1,0:T(8,128)(2,1)}, u32[]{:S(2)}) copy-start(bf16[128,2048]{1,0:T(8,128)(2,1)} %param.11) | copy-start | bytes 1572868
  184.3 18.3 %all-to-all-start.1 = ((bf16[16,2,8192]{2,1,0:T(2,128)(2,1)}), bf16[16,2,8192]{2,1,0:T(2,128)(2,1)S(1)}, u32[]{:S(2)}, u32[]{:S(2)}) async-start(bf16[16,2,8192]{2,1,0:T(2,128)(2,1)} %reshape.116), calls=%async_computation.1 | async-start | bytes 1048576 | tf_op jit(solution)/shard_map/all_to_all | solution.py:132
  188.2 25.5 %all-gather.3.cloned.1.call-start = ((), (), s32[]{:S(2)}) async-start(), calls=%async_computation.2 | async-start | bytes 1572864 | tf_op jit(solution)/shard_map/all_gather | solution.py:140
  203.3 0.7 copy-start.4
  206.3 203.0 %all-gather.5.cloned.1.call-start = ((), (), s32[]{:S(2)}) async-start(), calls=%async_computation.3 | async-start | bytes 17825792 | tf_op jit(solution)/shard_map/all_gather | solution.py:143
Sparse Core Ops, SparseCore 0:
  206.4 7.2 all-gather.2
  216.5 192.7 all-gather.4
where the time goes:
time: 432 us; the launch traced here: 426 us
  waiting for transfers between devices  226 us (52%)
  matrix products  83.5 us (19%)
  local copies, waits for them, and re-layouts  70 us (16%)
  other arithmetic  16.9 us (4%)
  starting transfers between devices  15.3 us (4%)
  between operations  14.1 us (3%)
    all_gather x1, waiting for transfers between devices, shards(): lax.all_gather(out_weight, 'ctx', axis=0, tiled=True)  196 us
    dot_general x12, matrix products, right_mul(): jnp.einsum('ckn,nq->ckq', signal, matrix, precision=lax.Precision.HIGHEST)  37.2 us
    dot_general x6, matrix products, left_mul(): jnp.einsum('kn,cnq->ckq', matrix, signal, precision=lax.Precision.HIGHEST)  31.4 us
    reshape x1, local copies, waits for them, and re-layouts, toeplitz(): jnp.tile(band_line, (1, width))[:, :width * row_span]  30.9 us
    unnamed x17, local copies, waits for them, and re-layouts  15.6 us
    all_to_all x1, waiting for transfers between devices, shards(): lax.all_to_all(long_part.reshape(1, per_dev, seq_len), 'ctx', split_axis=...  14.1 us
    unnamed x1, other arithmetic  11.8 us
    dot_general x1, matrix products, shards(): lax.dot_general(features, lax.all_gather(out_weight, 'ctx', axis=0, tiled...  9.26 us
  transfers between devices with their start and end apart: 5, of which 4 were waited for; matrix products, arithmetic and copies ran while one was open for 14% of the time, Pallas kernels for 0%

commit v1 on v0

v1 whole, which is shorter than its diff:
```python
import functools

import jax
import jax.numpy as jnp
from jax import lax
from jax.experimental import pallas as pl
from jax.experimental.pallas import tpu as pltpu
from jax.sharding import PartitionSpec as P


def short_kernel(group_size, own_ref, prior_ref, gate_ref, taps_ref, mid_ref):
    rows, lanes = own_ref.shape
    tap_count = taps_ref.shape[1]
    row_at = lax.broadcasted_iota(jnp.int32, (rows, tap_count), 0)
    lane_at = lax.broadcasted_iota(jnp.int32, (rows, tap_count), 1)
    before = lane_at > row_at
    window = jnp.concatenate([prior_ref[...], own_ref[...]], 0)
    group_at = lax.broadcasted_iota(jnp.int32, (rows, lanes), 1) // group_size
    total = jnp.zeros((rows, lanes), jnp.float32)
    for group in range(lanes // group_size):
        line = jnp.broadcast_to(taps_ref[group : group + 1, :], (rows, tap_count))
        turned = pltpu.roll(line, 0, 1, stride=1, stride_axis=0)
        band = jnp.concatenate(
            [jnp.where(before, turned, 0.0), jnp.where(before, 0.0, turned)], 1
        ).astype(jnp.bfloat16)
        part = jnp.dot(band, window, preferred_element_type=jnp.float32)
        total = jnp.where(group_at == group, part, total)
    mid = gate_ref[...].astype(jnp.float32) * total
    mid_ref[...] = mid.T.astype(jnp.bfloat16)


def short_conv(product, prior, gate_short, short_filter):
    rows, channels = product.shape
    groups, tap_count = short_filter.shape
    group_size = channels // groups
    lanes = min(128, channels)
    taps = jnp.roll(short_filter[:, ::-1], 1, axis=1).astype(jnp.float32)
    block = pl.BlockSpec((rows, lanes), lambda i: (0, i))
    return pl.pallas_call(
        functools.partial(short_kernel, group_size),
        grid=(channels // lanes,),
        in_specs=[block, block, block, pl.BlockSpec((lanes // group_size, tap_count), lambda i: (i, 0))],
        out_specs=pl.BlockSpec((lanes, rows), lambda i: (i, 0)),
        out_shape=jax.ShapeDtypeStruct((channels, rows), jnp.bfloat16),
        cost_estimate=pl.CostEstimate(
            flops=4 * groups * rows * tap_count * lanes, bytes_accessed=8 * rows * channels, transcendentals=0
        ),
        name="short_conv",
    )(product, prior, gate_short, taps)


def long_kernel(x_ref, h_ref, gate_ref, skip_ref, out_ref):
    batch, blocks, width = x_ref.shape
    half = width // 2
    row_at = lax.broadcasted_iota(jnp.int32, (half, width), 0)
    lane_at = lax.broadcasted_iota(jnp.int32, (half, width), 1)
    after = lane_at >= row_at
    low = lax.broadcasted_iota(jnp.int32, (blocks, width), 1) < half
    first = lax.broadcasted_iota(jnp.int32, (blocks, width), 0) < 1
    deep_at = lax.broadcasted_iota(jnp.int32, (2 * batch, blocks, width), 1)
    signals = [x_ref[c].astype(jnp.float32) for c in range(batch)]
    pieces = []
    zero = jnp.zeros((blocks, width), jnp.float32)
    for c in range(batch):
        swapped = pltpu.roll(signals[c], half, 1)
        even = signals[c] if c % 2 == 0 else swapped
        odd = swapped if c % 2 == 0 else signals[c]
        keep = low if c % 2 == 0 else jnp.logical_not(low)
        for piece in (even, odd):
            spread = [zero] * (batch // 2)
            spread[c // 2] = jnp.where(keep, piece, 0.0)
            pieces.append(jnp.concatenate(spread, 1))
    left = jnp.concatenate(pieces, 0).astype(jnp.bfloat16)
    filters = [h_ref[c].astype(jnp.float32) for c in range(batch)]
    previous = [jnp.zeros((half, width), jnp.float32)] * batch
    total = jnp.zeros((2 * batch, blocks, width), jnp.float32)
    for p in range(blocks):
        rows = []
        for c in range(batch):
            line = jnp.broadcast_to(filters[c][p : p + 1, :], (half, width))
            turned = pltpu.roll(line, 0, 1, stride=1, stride_axis=0)
            rows.append(jnp.where(after, turned, previous[c]))
            previous[c] = turned
        right = jnp.concatenate(rows, 0).astype(jnp.bfloat16)
        part = jnp.dot(left, right, preferred_element_type=jnp.float32)
        part = part.reshape(2 * batch, blocks, width)
        if p:
            part = jnp.where(deep_at >= p, pltpu.roll(part, p, 1), 0.0)
        total = total + part
    for c in range(batch):
        even, odd = total[2 * c], total[2 * c + 1]
        later = jnp.where(first, 0.0, pltpu.roll(odd, 1, 0))
        result = even + pltpu.roll(jnp.where(low, odd, later), half, 1)
        result = result.astype(jnp.bfloat16).astype(jnp.float32)
        gain = jnp.broadcast_to(skip_ref[c], (blocks, width))
        out_ref[c] = (gate_ref[c].astype(jnp.float32) * (result + gain * signals[c])).astype(jnp.bfloat16)


def long_conv(signals, filters, gates, gains):
    channels, blocks, width = signals.shape
    batch = 4
    block = pl.BlockSpec((batch, blocks, width), lambda i: (i, 0, 0))
    wide_gain = jnp.broadcast_to(gains[:, None, None], (channels, 1, width))
    return pl.pallas_call(
        long_kernel,
        grid=(channels // batch,),
        in_specs=[block, block, block, pl.BlockSpec((batch, 1, width), lambda i: (i, 0, 0))],
        out_specs=block,
        out_shape=jax.ShapeDtypeStruct(signals.shape, jnp.bfloat16),
        cost_estimate=pl.CostEstimate(
            flops=4 * channels * blocks * blocks * width * width,
            bytes_accessed=8 * channels * blocks * width,
            transcendentals=0,
        ),
        name="long_conv",
    )(signals, filters, gates, wide_gain)


def shards(
    value_in, key_in, gate_short, gate_long, short_filter, long_filter, skip_gain, out_weight
):
    tok_rows, channels = value_in.shape
    ctx_ways, ch_ways = lax.axis_size("ctx"), lax.axis_size("ch")
    per_dev = channels // ctx_ways
    inner = 2 ** ((ctx_ways.bit_length() - 1) // 2)
    outer = ctx_ways // inner
    lines = [[inner * m + g for m in range(outer)] for g in range(inner)]
    planes = [[inner * m + g for g in range(inner)] for m in range(outer)]
    owned = [
        ch_ways * (inner * (m // ch_ways) + g) + m % ch_ways for m in range(outer) for g in range(inner)
    ]

    def spread(by_channel):
        blocks = by_channel.reshape(outer // ch_ways, inner, ch_ways, per_dev, tok_rows)
        blocks = blocks.transpose(0, 2, 1, 3, 4).reshape(ctx_ways, per_dev, tok_rows)
        sent = lax.all_to_all(blocks, "ctx", split_axis=0, concat_axis=0, tiled=True)
        return sent.transpose(1, 0, 2)

    weights = lax.all_gather(out_weight, "ctx", axis=0, tiled=True, axis_index_groups=lines)
    product = (value_in.astype(jnp.float32) * key_in.astype(jnp.float32)).astype(jnp.bfloat16)
    prior = lax.ppermute(product, "ctx", [(s, s + 1) for s in range(ctx_ways - 1)])
    filters = lax.ppermute(
        long_filter.astype(jnp.bfloat16), "ctx", [(source, at) for at, source in enumerate(owned)]
    ).reshape(per_dev, ctx_ways, tok_rows)
    gates = spread(gate_long.T)
    signals = spread(short_conv(product, prior, gate_short, short_filter))
    me = lax.axis_index("ctx")
    line_at, place = me // inner, me % inner
    own_block = ch_ways * (inner * (line_at // ch_ways) + place) + line_at % ch_ways
    gains = lax.dynamic_slice_in_dim(skip_gain, own_block * per_dev, per_dev)
    gated = long_conv(signals, filters, gates, gains).transpose(1, 0, 2)
    gated = lax.all_to_all(
        gated.reshape(outer, inner, per_dev, tok_rows),
        "ctx",
        split_axis=0,
        concat_axis=0,
        axis_index_groups=lines,
        tiled=True,
    )
    gated = lax.all_gather(gated, "ch", axis=0, tiled=False)
    features = gated.transpose(2, 4, 0, 1, 3).reshape(inner * tok_rows, ch_ways * outer * per_dev)
    partial = jnp.dot(features, weights, preferred_element_type=jnp.float32).astype(jnp.bfloat16)
    partial = lax.all_to_all(
        partial.reshape(inner, tok_rows, channels),
        "ctx",
        split_axis=0,
        concat_axis=0,
        axis_index_groups=planes,
        tiled=True,
    )
    return partial.astype(jnp.float32).sum(0).astype(jnp.bfloat16)


def solution(mesh):
    in_specs = (
        P("ctx", "ch"),
        P("ctx", "ch"),
        P("ctx", "ch"),
        P("ctx", "ch"),
        P("ch", None),
        P(("ch", "ctx"), None),
        P("ch"),
        P("ctx", "ch"),
    )
    out_specs = P("ctx", "ch")
    return jax.shard_map(shards, mesh=mesh, in_specs=in_specs, out_specs=out_specs, check_vma=False)
```

time: 432 us -> 276 us (0.64)
  waiting for transfers between devices: 226 us -> 123 us
  matrix products: 83.5 us -> 4.52 us
  blocking collectives: 0 us -> 55.4 us
  local copies, waits for them, and re-layouts: 70 us -> 14.7 us
  Pallas kernels: 0 us -> 35.1 us
  other arithmetic: 16.9 us -> 3.49 us
  starting transfers between devices: 15.3 us -> 22.9 us
    all_gather x2, waiting for transfers between devices: 202 us -> 97.2 us  [the longest x1 81.1 us: shards(): lax.all_gather(out_weight, 'ctx', axis=0, tiled=True, axis_index_groups=l...]
    dot_general x20 -> x1, matrix products: 83.5 us -> 4.52 us  [shards(): jnp.dot(features, weights, preferred_element_type=jnp.float32)]
    all_to_all x0 -> x2, blocking collectives: none -> 55.4 us  [the longest x1 28.8 us: shards(): lax.all_to_all(partial.reshape(inner, tok_rows, channels), 'ctx', split_a...]
    pallas_call x0 -> x2, Pallas kernels: none -> 35.1 us  [the longest x1 24 us: long_conv(): pl.pallas_call(long_kernel, grid=(channels // batch,), in_specs=[block, b...]
    reshape x4, local copies, waits for them, and re-layouts: 39.3 us -> 4.56 us  [the longest x2 2.58 us: spread(): by_channel.reshape(outer // ch_ways, inner, ch_ways, per_dev, tok_rows)]
    unnamed x17 -> x9, local copies, waits for them, and re-layouts: 15.6 us -> 1.71 us
    ppermute x1 -> x2, waiting for transfers between devices: 0.01 us -> 13.2 us  [the longest x1 13.2 us: shards(): lax.ppermute(product, 'ctx', [(s, s + 1) for s in range(ctx_ways - 1)])]
    unnamed x1 -> x0, other arithmetic: 11.8 us -> none
  transfers between devices with their start and end apart: 5 -> 6, of which waited for: 4 -> 4; matrix products, arithmetic and copies ran while one was open for 14% -> 3% of each run, Pallas kernels for 0% -> 4%
where the time goes in v1:
time: 276 us; the launch traced here: 272 us
  waiting for transfers between devices  123 us (45%)
  blocking collectives  55.4 us (20%)
  Pallas kernels  35.1 us (13%)
  starting transfers between devices  22.9 us (8%)
  local copies, waits for them, and re-layouts  14.7 us (5%)
  between operations  13.6 us (5%)
  matrix products  4.52 us (2%)
  other arithmetic  3.49 us (1%)
    all_gather x1, waiting for transfers between devices, shards(): lax.all_gather(out_weight, 'ctx', axis=0, tiled=True, axis_index_groups=l...  81.1 us
    all_to_all x1, blocking collectives, shards(): lax.all_to_all(partial.reshape(inner, tok_rows, channels), 'ctx', split_a...  28.8 us
    all_to_all x1, blocking collectives, shards(): lax.all_to_all(gated.reshape(outer, inner, per_dev, tok_rows), 'ctx', spl...  26.6 us
    pallas_call x1, Pallas kernels, long_conv(): pl.pallas_call(long_kernel, grid=(channels // batch,), in_specs=[block, b...  24 us
    all_to_all x2, starting transfers between devices, spread(): lax.all_to_all(blocks, 'ctx', split_axis=0, concat_axis=0, tiled=True)  18.3 us
    all_gather x1, waiting for transfers between devices, shards(): gated = lax.all_gather(gated, 'ch', axis=0, tiled=False)  16.2 us
    ppermute x1, waiting for transfers between devices, shards(): lax.ppermute(product, 'ctx', [(s, s + 1) for s in range(ctx_ways - 1)])  13.2 us
    all_to_all x2, waiting for transfers between devices, spread(): lax.all_to_all(blocks, 'ctx', split_axis=0, concat_axis=0, tiled=True)  11.6 us
  transfers between devices with their start and end apart: 6, of which 4 were waited for; matrix products, arithmetic and copies ran while one was open for 3% of the time, Pallas kernels for 4%

profile of v1, /device:TPU:0, one launch (start us, length us, event | category | flops | bytes accessed | tf_op | source)
XLA Modules:
  0.0 272.5 jit_solution(14232767641707226147)
XLA Ops:
  6.5 0.0 copy-start.2
  6.5 1.4 reshape.30
  7.9 1.2 copy.22
  9.1 8.3 %all-to-all-start.1 = ((bf16[16,128,128]{2,1,0:T(8,128)(2,1)}), bf16[16,128,128]{2,1,0:T(8,128)(2,1)S(1)}, u32[]{:S(2)}, u32[]{:S(2)}) async-start(bf16[16,128,128]{2,1,0:T(8,128)(2,1)} %bitcast.6), calls=%async_computation.1 | async-start | bytes 1048576 | tf_op jit(solution)/shard_map/all_to_all | solution.py:136
  17.4 0.0 copy-start
  17.5 1.4 multiply_convert_fusion.own_ref
  18.9 0.0 copy-start.1
  18.9 3.9 %collective-permute-start = (bf16[128,2048]{1,0:T(8,128)(2,1)S(1)}, bf16[128,2048]{1,0:T(8,128)(2,1)S(1)}, u32[]{:S(2)}, u32[]{:S(2)}) collective-permute-start(bf16[128,2048]{1,0:T(8,128)(2,1)S(1)} %multiply_convert_fusion.own_ref), channel_id=1, source_target_pairs={{0,2},{2,4},{4,6},{6,8},{8,10},{10,12},{12,14},{14,16},{16,18},{18... | collective-permute-start | bytes 1572872 | tf_op jit(solution)/shard_map/ppermute | solution.py:141
  22.8 0.0 copy-done.2
  22.8 0.1 slice.13
  22.8 0.1 slice.14
  22.9 0.7 maximum_convert_fusion.taps_ref
  23.6 13.2 %collective-permute-done.prior_ref = bf16[128,2048]{1,0:T(8,128)(2,1)S(1)} collective-permute-done((bf16[128,2048]{1,0:T(8,128)(2,1)S(1)}, bf16[128,2048]{1,0:T(8,128)(2,1)S(1)}, u32[]{:S(2)}, u32[]{:S(2)}) %collective-permute-start) | collective-permute-done | bytes 524320 | tf_op jit(solution)/shard_map/ppermute | solution.py:141
  36.8 0.0 copy-done.1
  36.8 0.0 copy-start.3
  36.8 0.8 copy-done.3
  37.6 11.1 %short_conv.1 = bf16[2048,128]{1,0:T(8,128)(2,1)} custom-call(bf16[128,2048]{1,0:T(8,128)(2,1)} %copy-done.1, bf16[128,2048]{1,0:T(8,128)(2,1)} %copy-done.3, bf16[128,2048]{1,0:T(8,128)(2,1)} %gate_ref.1, f32[128,128]{1,0:T(8,128)} %maximum_convert_fusion.taps_ref), custom_call_target="tpu_custom_call" | custom-call | flops 1073741824 | bytes 2097152 | tf_op jit(solution)/shard_map/short_conv/pallas_call | solution.py:39
  48.7 1.9 copy.20
  50.6 0.0 all-to-all-done.1
  50.6 10.0 %all-to-all-start = ((bf16[16,128,128]{2,1,0:T(8,128)(2,1)}), bf16[16,128,128]{2,1,0:T(8,128)(2,1)S(1)}, u32[]{:S(2)}, u32[]{:S(2)}) async-start(bf16[16,128,128]{2,1,0:T(8,128)(2,1)} %bitcast.2), calls=%async_computation | async-start | bytes 1048576 | tf_op jit(solution)/shard_map/all_to_all | solution.py:136
  60.6 0.0 all-gather.6.cloned.1.call-start
  60.7 0.0 copy-done
  60.7 0.1 convert_element_type.24
  60.7 0.7 collective-permute-start.1
  61.5 0.8 dynamic_slice.3
  62.3 0.0 collective-permute-done.1
  62.3 0.9 copy.27
  63.2 1.1 copy.30
  64.3 11.6 %all-to-all-done = bf16[16,128,128]{2,1,0:T(8,128)(2,1)S(1)} async-done(((bf16[16,128,128]{2,1,0:T(8,128)(2,1)}), bf16[16,128,128]{2,1,0:T(8,128)(2,1)S(1)}, u32[]{:S(2)}, u32[]{:S(2)}) %all-to-all-start) | async-done | bytes 524320 | tf_op jit(solution)/shard_map/all_to_all | solution.py:136
  75.9 1.1 copy.31
  77.0 0.8 broadcast_in_dim.2.skip_ref
  77.8 24.0 %long_conv.1 = bf16[128,16,128]{2,1,0:T(8,128)(2,1)} custom-call(bf16[128,16,128]{2,1,0:T(8,128)(2,1)} %bitcast.34, bf16[128,16,128]{2,1,0:T(8,128)(2,1)} %bitcast.32, bf16[128,16,128]{2,1,0:T(8,128)(2,1)} %bitcast.33, f32[128,1,128]{2,1,0:T(1,128)} %broadcast_in_dim.2.skip_ref), custom_call_target="tpu_custom_call" | custom-call | flops 2147483648 | bytes 2097152 | tf_op jit(solution)/shard_map/long_conv/pallas_call | solution.py:104
  101.8 1.2 copy.24
  103.0 26.6 %all_to_all.20 = bf16[4,4,128,128]{3,1,2,0:T(4,128)(2,1)S(1)} all-to-all(bf16[4,4,128,128]{3,1,2,0:T(4,128)(2,1)S(1)} %copy.24), channel_id=1, replica_groups={{0,8,16,24},{2,10,18,26},{4,12,20,28},{6,14,22,30},{1,9,17,25},{3,11,19..., dimensions={0} | all-to-all | bytes 1048576 | tf_op jit(solution)/shard_map/all_to_all | solution.py:152
  129.6 0.9 copy.25
  130.5 0.0 all-gather.6.cloned.1.call-update
  130.5 0.0 all-gather.4.cloned.1.call-start
  130.6 0.7 all-gather.4.cloned.1.call-update
  131.3 16.2 %all-gather.6.cloned.1.call-done = bf16[8,4,128,128]{3,2,1,0:T(8,128)(2,1)} async-done(((bf16[4,4,128,128]{3,2,1,0:T(8,128)(2,1)}), bf16[8,4,128,128]{3,2,1,0:T(8,128)(2,1)}) %all-gather.6.cloned.1.call-update) | async-done | bytes 1048592 | tf_op jit(solution)/shard_map/all_gather | solution.py:160
  147.4 1.7 copy.26
  149.1 0.8 reshape.33
  149.9 81.1 %all-gather.4.cloned.1.call-done = bf16[1024,2048]{1,0:T(8,128)(2,1)} async-done(((bf16[256,2048]{1,0:T(8,128)(2,1)}), bf16[1024,2048]{1,0:T(8,128)(2,1)}) %all-gather.4.cloned.1.call-update) | async-done | bytes 4194320 | tf_op jit(solution)/shard_map/all_gather | solution.py:139
  231.0 4.5 %convolution_convert_fusion = bf16[512,2048]{1,0:T(8,128)(2,1)S(1)} fusion(bf16[512,1024]{1,0:T(8,128)(2,1)S(1)} %reshape.33, bf16[1024,2048]{1,0:T(8,128)(2,1)} %all-gather.4.cloned.1.call-done), kind=kOutput, calls=%fused_computation | convolution fusion | flops 2148532224 | bytes 7340032 | tf_op jit(solution)/shard_map/dot_general | solution.py:162
  235.5 28.8 %all_to_all.21 = bf16[4,128,2048]{2,1,0:T(8,128)(2,1)S(1)} all-to-all(bf16[4,128,2048]{2,1,0:T(8,128)(2,1)S(1)} %bitcast.28), channel_id=1, replica_groups={{0,2,4,6},{8,10,12,14},{16,18,20,22},{24,26,28,30},{1,3,5,7},{9,11,13,1..., dimensions={0} | all-to-all | bytes 4194304 | tf_op jit(solution)/shard_map/all_to_all | solution.py:163
  264.3 1.3 reduce_sum.12
Async XLA Ops:
  6.5 16.2 %copy-start.2 = (bf16[128,128]{1,0:T(8,128)(2,1)S(1)}, bf16[128,128]{1,0:T(8,128)(2,1)}, u32[]{:S(2)}) copy-start(bf16[128,128]{1,0:T(8,128)(2,1)} %param.12) | copy-start | bytes 98308
  9.1 41.5 %all-to-all-start.1 = ((bf16[16,128,128]{2,1,0:T(8,128)(2,1)}), bf16[16,128,128]{2,1,0:T(8,128)(2,1)S(1)}, u32[]{:S(2)}, u32[]{:S(2)}) async-start(bf16[16,128,128]{2,1,0:T(8,128)(2,1)} %bitcast.6), calls=%async_computation.1 | async-start | bytes 1048576 | tf_op jit(solution)/shard_map/all_to_all | solution.py:136
  17.4 43.2 %copy-start = (f32[128,2048]{1,0:T(8,128)S(1)}, f32[128,2048]{1,0:T(8,128)}, u32[]{:S(2)}) copy-start(f32[128,2048]{1,0:T(8,128)} %param.13) | copy-start | bytes 3145732
  18.9 18.0 %copy-start.1 = (bf16[128,2048]{1,0:T(8,128)(2,1)}, bf16[128,2048]{1,0:T(8,128)(2,1)S(1)}, u32[]{:S(2)}) copy-start(bf16[128,2048]{1,0:T(8,128)(2,1)S(1)} %multiply_convert_fusion.own_ref) | copy-start | bytes 1572868
  18.9 17.9 %collective-permute-start = (bf16[128,2048]{1,0:T(8,128)(2,1)S(1)}, bf16[128,2048]{1,0:T(8,128)(2,1)S(1)}, u32[]{:S(2)}, u32[]{:S(2)}) collective-permute-start(bf16[128,2048]{1,0:T(8,128)(2,1)S(1)} %multiply_convert_fusion.own_ref), channel_id=1, source_target_pairs={{0,2},{2,4},{4,6},{6,8},{8,10},{10,12},{12,14},{14,16},{16,18},{18... | collective-permute-start | bytes 1572872 | tf_op jit(solution)/shard_map/ppermute | solution.py:141
  36.8 0.8 copy-start.3
  50.6 25.3 %all-to-all-start = ((bf16[16,128,128]{2,1,0:T(8,128)(2,1)}), bf16[16,128,128]{2,1,0:T(8,128)(2,1)S(1)}, u32[]{:S(2)}, u32[]{:S(2)}) async-start(bf16[16,128,128]{2,1,0:T(8,128)(2,1)} %bitcast.2), calls=%async_computation | async-start | bytes 1048576 | tf_op jit(solution)/shard_map/all_to_all | solution.py:136
  60.6 86.8 %all-gather.6.cloned.1.call-start = ((), (), s32[]{:S(2)}) async-start(), calls=%async_computation.5 | async-start | bytes 1572864 | tf_op jit(solution)/shard_map/all_gather | solution.py:160
  60.7 1.5 collective-permute-start.1
  130.5 100.5 %all-gather.4.cloned.1.call-start = ((), (), s32[]{:S(2)}) async-start(), calls=%async_computation.4 | async-start | bytes 5242880 | tf_op jit(solution)/shard_map/all_gather | solution.py:139
Sparse Core Ops, SparseCore 0:
  130.6 16.7 all-gather.5
  149.0 81.9 all-gather.3

commit v2 on v1

v2 whole, which is shorter than its diff:
```python
import functools

import jax
import jax.numpy as jnp
from jax import lax
from jax.experimental import pallas as pl
from jax.experimental.pallas import tpu as pltpu
from jax.sharding import PartitionSpec as P

MESH = pl.DeviceIdType.MESH
F32, BF16 = jnp.float32, jnp.bfloat16


def remote(src, dst, send_sem, recv_sem, ctx, ch=None):
    ch = lax.axis_index("ch") if ch is None else ch
    return pltpu.make_async_remote_copy(
        src_ref=src, dst_ref=dst, send_sem=send_sem, recv_sem=recv_sem, device_id=(ctx, ch), device_id_type=MESH
    )


def short_tile(group_size, own, prior, gate, taps_ref, first_group):
    rows, lanes = own.shape
    tap_count = taps_ref.shape[2]
    row_at = lax.broadcasted_iota(jnp.int32, (rows, tap_count), 0)
    lane_at = lax.broadcasted_iota(jnp.int32, (rows, tap_count), 1)
    before = lane_at > row_at
    window = jnp.concatenate([prior, own], 0)
    group_at = lax.broadcasted_iota(jnp.int32, (rows, lanes), 1) // group_size
    total = jnp.zeros((rows, lanes), F32)
    for group in range(lanes // group_size):
        line = jnp.broadcast_to(taps_ref[first_group + group], (rows, tap_count))
        turned = pltpu.roll(line, 0, 1, stride=1, stride_axis=0)
        band = jnp.concatenate([jnp.where(before, turned, 0.0), jnp.where(before, 0.0, turned)], 1).astype(BF16)
        part = jnp.dot(band, window, preferred_element_type=F32)
        total = jnp.where(group_at == group, part, total)
    return (gate.astype(F32) * total).T


def long_quad(batch, start, xs, hs, gs, skip_ref, skip_at, out):
    _, blocks, width = xs.shape
    half = width // 2
    row_at = lax.broadcasted_iota(jnp.int32, (half, width), 0)
    lane_at = lax.broadcasted_iota(jnp.int32, (half, width), 1)
    after = lane_at >= row_at
    low = lax.broadcasted_iota(jnp.int32, (blocks, width), 1) < half
    first = lax.broadcasted_iota(jnp.int32, (blocks, width), 0) < 1
    deep_at = lax.broadcasted_iota(jnp.int32, (2 * batch, blocks, width), 1)
    signals = [xs[start + c] for c in range(batch)]
    pieces = []
    zero = jnp.zeros((blocks, width), F32)
    for c in range(batch):
        swapped = pltpu.roll(signals[c], half, 1)
        even = signals[c] if c % 2 == 0 else swapped
        odd = swapped if c % 2 == 0 else signals[c]
        keep = low if c % 2 == 0 else jnp.logical_not(low)
        for piece in (even, odd):
            spread = [zero] * (batch // 2)
            spread[c // 2] = jnp.where(keep, piece, 0.0)
            pieces.append(jnp.concatenate(spread, 1))
    left = jnp.concatenate(pieces, 0).astype(BF16)
    previous = [jnp.zeros((half, width), F32)] * batch
    total = jnp.zeros((2 * batch, blocks, width), F32)
    for p in range(blocks):
        rows = []
        for c in range(batch):
            line = jnp.broadcast_to(hs[start + c, :, p * width : (p + 1) * width], (half, width))
            turned = pltpu.roll(line, 0, 1, stride=1, stride_axis=0)
            rows.append(jnp.where(after, turned, previous[c]))
            previous[c] = turned
        right = jnp.concatenate(rows, 0).astype(BF16)
        part = jnp.dot(left, right, preferred_element_type=F32)
        part = part.reshape(2 * batch, blocks, width)
        if p:
            part = jnp.where(deep_at >= p, pltpu.roll(part, p, 1), 0.0)
        total = total + part
    for c in range(batch):
        even, odd = total[2 * c], total[2 * c + 1]
        later = jnp.where(first, 0.0, pltpu.roll(odd, 1, 0))
        result = even + pltpu.roll(jnp.where(low, odd, later), half, 1)
        result = result.astype(BF16).astype(F32)
        gain = jnp.broadcast_to(skip_ref[skip_at + start + c], (blocks, width))
        out[start + c] = gs[start + c] * (result + gain * signals[c])


def kernel(
    sizes,
    value_ref, key_ref, gate_s_ref, gate_l_ref, taps_ref, filt_ref, skip_ref, w_ref,
    out_ref,
    prod, prior, mid_send, gate_send, filt_send, mid_in, gate_in, filt_in, gated, feat, wbuf,
    part_send, part_in, own_part, xs, hs, gs, ys,
    halo_sem, filt_sem, mid_s, mid_r, gate_s, gate_r, feat_s, feat_r, w_own, w_right, w_left, w_recv, part_s, part_r,
):
    ctx_ways, ch_ways, outer, inner, per_dev, group_size = sizes
    rows, channels = value_ref.shape
    me, core = lax.axis_index("ctx"), lax.axis_index("ch")
    line_at, place = me // inner, me % inner

    def owned(d):
        m, g = d // inner, d % inner
        return ch_ways * (inner * (m // ch_ways) + g) + m % ch_ways

    def owner_of(block):
        m_hi, g, e = block // (ch_ways * inner), (block // ch_ways) % inner, block % ch_ways
        return inner * (ch_ways * m_hi + e) + g

    barrier = pltpu.get_barrier_semaphore()

    @pl.loop(1, ctx_ways)
    def _(s):
        pl.semaphore_signal(barrier, inc=1, device_id=((me + s) % ctx_ways, core), device_id_type=MESH)

    for other in range(1, ch_ways):

        @pl.loop(0, outer)
        def _(m):
            pl.semaphore_signal(
                barrier, inc=1, device_id=(m * inner + place, (core + other) % ch_ways), device_id_type=MESH
            )

    prod[...] = (value_ref[...].astype(F32) * key_ref[...].astype(F32)).astype(BF16)
    filt_send[...] = filt_ref[...].astype(BF16)
    pl.semaphore_wait(barrier, ctx_ways - 1 + (ch_ways - 1) * outer)

    halo = remote(prod, prior, halo_sem.at[0], halo_sem.at[1], (me + 1) % ctx_ways)

    @pl.when(me < ctx_ways - 1)
    def _():
        halo.start()

    filt_to = owner_of(me)
    filt_copy = remote(filt_send, filt_in, filt_sem.at[0], filt_sem.at[1], filt_to)

    @pl.when(filt_to != me)
    def _():
        filt_copy.start()

    own_w = pltpu.make_async_copy(w_ref, wbuf.at[line_at], w_own)
    own_w.start()

    def right_copy(s):
        at = jnp.maximum(line_at - s, 0)
        src = w_ref if s == 0 else wbuf.at[at]
        return remote(src, wbuf.at[at], w_right.at[s], w_recv.at[at], (me + inner) % ctx_ways)

    def left_copy(s):
        at = jnp.minimum(line_at + s, outer - 1)
        src = w_ref if s == 0 else wbuf.at[at]
        return remote(src, wbuf.at[at], w_left.at[s], w_recv.at[at], (me + ctx_ways - inner) % ctx_ways)

    def right_on(s):
        return jnp.logical_and(line_at >= s, line_at < outer - 1)

    def left_on(s):
        return jnp.logical_and(line_at + s < outer, line_at > 0)

    def w_step(s):
        @pl.when(right_on(s))
        def _():
            copy = right_copy(s)
            if s:
                copy.wait_recv()
            copy.start()

        @pl.when(left_on(s))
        def _():
            copy = left_copy(s)
            if s:
                copy.wait_recv()
            copy.start()

    w_step(0)

    lanes = min(128, channels)
    in_tile = lanes // per_dev
    tiles = channels // lanes

    def block_copy(buf, into, send, recv, block):
        return remote(buf.at[block], into.at[me], send.at[block], recv.at[me], owner_of(block))

    def send_tile(tile, values, buf, into, send, recv):
        buf[pl.ds(tile * in_tile, in_tile)] = values.reshape(in_tile, per_dev, rows).astype(BF16)
        for b in range(in_tile):
            block = tile * in_tile + b

            @pl.when(owner_of(block) != me)
            def _():
                block_copy(buf, into, send, recv, block).start()

    shift = owned(me) // in_tile

    @pl.loop(0, tiles)
    def _(t):
        tile = (t + shift + 1) % tiles
        at = pl.ds(pl.multiple_of(tile * lanes, lanes), lanes)
        send_tile(tile, gate_l_ref[:, at].astype(F32).T, gate_send, gate_in, gate_s, gate_r)

    @pl.when(me > 0)
    def _():
        halo.wait_recv()

    @pl.when(me == 0)
    def _():
        prior[...] = jnp.zeros_like(prior)

    @pl.loop(0, tiles)
    def _(t):
        tile = (t + shift + 1) % tiles
        at = pl.ds(pl.multiple_of(tile * lanes, lanes), lanes)
        groups = lanes // group_size
        values = short_tile(group_size, prod[:, at], prior[:, at], gate_s_ref[:, at], taps_ref, tile * groups)
        send_tile(tile, values, mid_send, mid_in, mid_s, mid_r)

    if outer > 2:
        w_step(1)

    mine = owned(me)
    gate_in[me] = gate_send[mine]
    mid_in[me] = mid_send[mine]

    @pl.when(filt_to != me)
    def _():
        filt_copy.wait_recv()

    @pl.when(filt_to == me)
    def _():
        filt_in[...] = filt_send[...]

    @pl.loop(1, ctx_ways)
    def _(s):
        a = (me + s) % ctx_ways
        remote(gate_send.at[0], gate_in.at[a], gate_s.at[0], gate_r.at[a], a).wait_recv()
        remote(mid_send.at[0], mid_in.at[a], mid_s.at[0], mid_r.at[a], a).wait_recv()

    step, batch = xs.shape[0], 4

    def long_step(i):
        at = pl.ds(pl.multiple_of(i * step, step), step)
        xs[...] = jnp.swapaxes(mid_in[:, at, :].astype(F32), 0, 1)
        gs[...] = jnp.swapaxes(gate_in[:, at, :].astype(F32), 0, 1)
        hs[...] = filt_in[at, :].astype(F32).reshape(hs.shape)

        @pl.loop(0, step // batch)
        def _(q):
            long_quad(batch, q * batch, xs, hs, gs, skip_ref, i * step, ys)

        gated[:, at, :] = jnp.swapaxes(ys[...], 0, 1).astype(BF16)

    long_steps = per_dev // step
    for s in range(2, outer - 1):
        low, high = (s - 2) * long_steps // (outer - 2), (s - 1) * long_steps // (outer - 2)

        @pl.loop(low, high)
        def _(i):
            long_step(i)

        w_step(s)

    done = (max(outer - 3, 0)) * long_steps // max(outer - 2, 1)

    @pl.loop(done, long_steps)
    def _(i):
        long_step(i)

    slot = core * outer + line_at

    def feat_copy(m, ch, n):
        return remote(
            gated.at[pl.ds(m * inner, inner)], feat.at[slot], feat_s.at[n], feat_r.at[slot], m * inner + place, ch
        )

    for k in range(ch_ways):

        @pl.loop(0, outer)
        def _(s):
            m, ch = (line_at + s) % outer, (core + k) % ch_ways

            @pl.when(jnp.logical_or(m != line_at, ch != core))
            def _():
                feat_copy(m, ch, ch * outer + m).start()

    feat[slot] = gated[pl.ds(me - place, inner)]

    own_w.wait()
    for s in range(1, outer):

        @pl.when(jnp.logical_and(line_at == outer - 1, line_at >= s))
        def _():
            right_copy(s).wait_recv()

        @pl.when(jnp.logical_and(line_at == 0, line_at + s < outer))
        def _():
            left_copy(s).wait_recv()

    @pl.loop(0, ch_ways * outer)
    def _(n):
        @pl.when(n != slot)
        def _():
            remote(
                gated.at[pl.ds(0, inner)], feat.at[n], feat_s.at[n], feat_r.at[n], (n % outer) * inner + place, n // outer
            ).wait_recv()

    depth = ch_ways * outer * per_dev

    def features(g):
        return feat[:, g].astype(F32).reshape(depth, rows).T.astype(BF16)

    cols = min(512, channels)

    @pl.loop(1, inner)
    def _(s):
        g = (place + s) % inner
        left = features(g)

        @pl.loop(0, channels // cols)
        def _(n):
            at = pl.ds(pl.multiple_of(n * cols, cols), cols)
            right = wbuf[:, :, at].reshape(depth, cols)
            part_send[g, :, at] = jnp.dot(left, right, preferred_element_type=F32).astype(BF16)

        remote(part_send.at[g], part_in.at[place], part_s.at[g], part_r.at[place], me - place + g).start()

    left = features(place)

    @pl.loop(0, channels // cols)
    def _(n):
        at = pl.ds(pl.multiple_of(n * cols, cols), cols)
        right = wbuf[:, :, at].reshape(depth, cols)
        own_part[:, at] = jnp.dot(left, right, preferred_element_type=F32)

    @pl.loop(1, inner)
    def _(s):
        g = (place + s) % inner
        remote(part_send.at[g], part_in.at[g], part_s.at[g], part_r.at[g], me - place + g).wait_recv()

        own_part[...] += part_in[g].astype(F32)

    out_ref[...] = own_part[...].astype(BF16)

    @pl.when(me < ctx_ways - 1)
    def _():
        halo.wait_send()

    @pl.when(filt_to != me)
    def _():
        filt_copy.wait_send()

    for s in range(outer - 1):

        @pl.when(right_on(s))
        def _():
            right_copy(s).wait_send()

        @pl.when(left_on(s))
        def _():
            left_copy(s).wait_send()

    @pl.loop(0, ctx_ways)
    def _(block):
        @pl.when(owner_of(block) != me)
        def _():
            block_copy(gate_send, gate_in, gate_s, gate_r, block).wait_send()
            block_copy(mid_send, mid_in, mid_s, mid_r, block).wait_send()

    @pl.loop(0, ch_ways * outer)
    def _(n):
        @pl.when(n != slot)
        def _():
            feat_copy(n % outer, n // outer, n).wait_send()

    @pl.loop(1, inner)
    def _(s):
        g = (place + s) % inner
        remote(part_send.at[g], part_in.at[place], part_s.at[g], part_r.at[place], me - place + g).wait_send()


def shards(
    value_in, key_in, gate_short, gate_long, short_filter, long_filter, skip_gain, out_weight
):
    rows, channels = value_in.shape
    ctx_ways, ch_ways = lax.axis_size("ctx"), lax.axis_size("ch")
    per_dev = channels // ctx_ways
    inner = 2 ** ((ctx_ways.bit_length() - 1) // 2)
    outer = ctx_ways // inner
    group_size = channels // short_filter.shape[0]
    taps = jnp.roll(short_filter[:, ::-1], 1, axis=1).astype(F32)[:, None, :]
    me = lax.axis_index("ctx")
    line_at, place = me // inner, me % inner
    own_block = ch_ways * (inner * (line_at // ch_ways) + place) + line_at % ch_ways
    gains = lax.dynamic_slice_in_dim(skip_gain, own_block * per_dev, per_dev)
    gains = jnp.broadcast_to(gains[:, None, None], (per_dev, 1, rows))
    step = min(16, per_dev)
    seq_len = ctx_ways * rows
    sizes = (ctx_ways, ch_ways, outer, inner, per_dev, group_size)
    blocks = pltpu.VMEM((ctx_ways, per_dev, rows), BF16)
    tokens = pltpu.VMEM((rows, channels), BF16)
    filt = pltpu.VMEM((per_dev, seq_len), BF16)
    lines = pltpu.VMEM((step, ctx_ways, rows), F32)
    dma = pltpu.SemaphoreType.DMA
    vmem = pl.BlockSpec(memory_space=pltpu.VMEM)
    return pl.pallas_call(
        functools.partial(kernel, sizes),
        out_shape=jax.ShapeDtypeStruct((rows, channels), BF16),
        in_specs=[vmem] * 7 + [pl.BlockSpec(memory_space=pl.ANY)],
        out_specs=vmem,
        scratch_shapes=[
            tokens, tokens, blocks, blocks, filt, blocks, blocks, filt, blocks,
            pltpu.VMEM((ch_ways * outer, inner, per_dev, rows), BF16),
            pltpu.VMEM((outer,) + out_weight.shape, BF16),
            pltpu.VMEM((inner, rows, channels), BF16),
            pltpu.VMEM((inner, rows, channels), BF16),
            pltpu.VMEM((rows, channels), F32),
            lines,
            pltpu.VMEM((step, 1, seq_len), F32),
            lines, lines,
            dma((2,)), dma((2,)),
            dma((ctx_ways,)), dma((ctx_ways,)), dma((ctx_ways,)), dma((ctx_ways,)),
            dma((ch_ways * outer,)), dma((ch_ways * outer,)),
            dma, dma((outer,)), dma((outer,)), dma((outer,)), dma((inner,)), dma((inner,)),
        ],
        compiler_params=pltpu.CompilerParams(
            collective_id=0, has_side_effects=True, vmem_limit_bytes=48 * 1024 * 1024
        ),
        name="hyena",
    )(value_in, key_in, gate_short, gate_long, taps, long_filter, gains, out_weight)


def solution(mesh):
    in_specs = (
        P("ctx", "ch"),
        P("ctx", "ch"),
        P("ctx", "ch"),
        P("ctx", "ch"),
        P("ch", None),
        P(("ch", "ctx"), None),
        P("ch"),
        P("ctx", "ch"),
    )
    out_specs = P("ctx", "ch")
    return jax.shard_map(shards, mesh=mesh, in_specs=in_specs, out_specs=out_specs, check_vma=False)
```

time: 276 us -> 164 us (0.59)
  waiting for transfers between devices: 123 us -> 0 us
  Pallas kernels: 35.1 us -> 154 us
  blocking collectives: 55.4 us -> 0 us
  starting transfers between devices: 22.9 us -> 0 us
  between operations: 13.6 us -> 0.07 us
  local copies, waits for them, and re-layouts: 14.7 us -> 7.91 us
  matrix products: 4.52 us -> 0 us
  other arithmetic: 3.49 us -> 0.21 us
    pallas_call x2 -> x1, Pallas kernels: 35.1 us -> 154 us  [shards(): pl.pallas_call(functools.partial(kernel, sizes), out_shape=jax.ShapeDtype...]
    all_gather x2 -> x0, waiting for transfers between devices: 97.2 us -> none  [the longest x1 81.1 us: shards(): lax.all_gather(out_weight, 'ctx', axis=0, tiled=True, axis_index_groups=l...]
    all_to_all x2 -> x0, blocking collectives: 55.4 us -> none  [the longest x1 28.8 us: shards(): lax.all_to_all(partial.reshape(inner, tok_rows, channels), 'ctx', split_a...]
    all_to_all x2 -> x0, starting transfers between devices: 18.3 us -> none  [spread(): lax.all_to_all(blocks, 'ctx', split_axis=0, concat_axis=0, tiled=True)]
    ppermute x2 -> x0, waiting for transfers between devices: 13.2 us -> none  [the longest x1 13.2 us: shards(): lax.ppermute(product, 'ctx', [(s, s + 1) for s in range(ctx_ways - 1)])]
    all_to_all x2 -> x0, waiting for transfers between devices: 11.6 us -> none  [spread(): lax.all_to_all(blocks, 'ctx', split_axis=0, concat_axis=0, tiled=True)]
    unnamed x9 -> x15, local copies, waits for them, and re-layouts: 1.71 us -> 6.37 us
    reshape x4 -> x0, local copies, waits for them, and re-layouts: 4.56 us -> none  [the longest x2 2.58 us: spread(): by_channel.reshape(outer // ch_ways, inner, ch_ways, per_dev, tok_rows)]
  transfers between devices with their start and end apart: 6 -> 0, of which waited for: 4 -> 0; matrix products, arithmetic and copies ran while one was open for 3% -> 0% of each run, Pallas kernels for 4% -> 0%
where the time goes in v2:
time: 164 us; the launch traced here: 162 us
  Pallas kernels  154 us (94%)
  local copies, waits for them, and re-layouts  7.91 us (5%)
    pallas_call x1, Pallas kernels, shards(): pl.pallas_call(functools.partial(kernel, sizes), out_shape=jax.ShapeDtype...  154 us
    unnamed x15, local copies, waits for them, and re-layouts  6.37 us

profile of v2, /device:TPU:0, one launch (start us, length us, event | category | flops | bytes accessed | tf_op | source)
XLA Modules:
  0.0 162.0 jit_solution(16199309206011959589)
XLA Ops:
  0.0 0.0 copy-start.6
  0.0 0.0 copy-start.2
  0.0 0.8 dynamic_slice.3
  0.8 0.0 copy-done.6
  0.8 0.1 slice_reduce_fusion
  0.9 0.1 slice.13
  1.0 0.1 slice.14
  1.1 0.1 copy.11
  1.2 0.2 concatenate.18
  1.4 0.2 maximum_convert_fusion.taps_ref
  1.6 0.2 broadcast_in_dim.2.skip_ref
  1.8 0.0 copy-done.2
  1.8 0.0 copy-start
  1.8 1.2 copy-done
  3.0 0.0 copy-start.1
  3.0 1.2 copy-done.1
  4.3 0.0 copy-start.3
  4.3 1.0 copy-done.3
  5.3 0.0 copy-start.4
  5.3 1.0 copy-done.4
  6.3 0.0 copy-start.5
  6.3 1.0 copy-done.5
  7.4 153.9 %hyena.1 = bf16[128,2048]{1,0:T(8,128)(2,1)S(1)} custom-call(bf16[128,2048]{1,0:T(8,128)(2,1)S(1)} %copy-done.2, bf16[128,2048]{1,0:T(8,128)(2,1)S(1)} %copy-done.3, bf16[128,2048]{1,0:T(8,128)(2,1)S(1)} %copy-done.4, bf16[128,2048]{1,0:T(8,128)(2,1)S(1)} %copy-done.5, f32[128,1,128]{2,1,0:T(1,128)S(1)} %maximum_convert_fusion.taps_ref, ...), custom_call_target="tpu_custom_call" | custom-call | tf_op jit(solution)/shard_map/hyena/pallas_call | solution.py:400
  161.3 0.8 copy.13
Async XLA Ops:
  0.0 0.8 copy-start.6
  0.0 1.8 %copy-start.2 = (bf16[128,2048]{1,0:T(8,128)(2,1)S(1)}, bf16[128,2048]{1,0:T(8,128)(2,1)}, u32[]{:S(2)}) copy-start(bf16[128,2048]{1,0:T(8,128)(2,1)} %value_ref.1) | copy-start | bytes 1572868
  1.8 1.2 copy-start
  3.0 1.2 copy-start.1
  4.3 1.0 copy-start.3
  5.3 1.0 copy-start.4
  6.3 1.0 copy-start.5

commit v3 on v2

--- a/solution.py
+++ b/solution.py
@@ -210,9 +210,6 @@
         values = short_tile(group_size, prod[:, at], prior[:, at], gate_s_ref[:, at], taps_ref, tile * groups)
         send_tile(tile, values, mid_send, mid_in, mid_s, mid_r)
 
-    if outer > 2:
-        w_step(1)
-
     mine = owned(me)
     gate_in[me] = gate_send[mine]
     mid_in[me] = mid_send[mine]
@@ -230,6 +227,9 @@
         a = (me + s) % ctx_ways
         remote(gate_send.at[0], gate_in.at[a], gate_s.at[0], gate_r.at[a], a).wait_recv()
         remote(mid_send.at[0], mid_in.at[a], mid_s.at[0], mid_r.at[a], a).wait_recv()
+
+    if outer > 2:
+        w_step(1)
 
     step, batch = xs.shape[0], 4
 

time: 164 us -> 171 us (1.043)
  Pallas kernels: 154 us -> 159 us
    pallas_call x1, Pallas kernels: 154 us -> 159 us  [shards(): pl.pallas_call(functools.partial(kernel, sizes), out_shape=jax.ShapeDtype...]
where the time goes in v3:
time: 171 us; the launch traced here: 168 us
  Pallas kernels  159 us (93%)
  local copies, waits for them, and re-layouts  7.91 us (5%)
    pallas_call x1, Pallas kernels, shards(): pl.pallas_call(functools.partial(kernel, sizes), out_shape=jax.ShapeDtype...  159 us
    unnamed x15, local copies, waits for them, and re-layouts  6.37 us

profile of v3, /device:TPU:0, one launch (start us, length us, event | category | flops | bytes accessed | tf_op | source)
XLA Modules:
  0.0 167.5 jit_solution(9618553112553415738)
XLA Ops:
  0.0 0.0 copy-start.6
  0.0 0.0 copy-start.2
  0.0 0.8 dynamic_slice.3
  0.8 0.0 copy-done.6
  0.8 0.1 slice_reduce_fusion
  0.9 0.1 slice.13
  1.0 0.1 slice.14
  1.1 0.1 copy.11
  1.2 0.2 concatenate.18
  1.4 0.2 maximum_convert_fusion.taps_ref
  1.6 0.2 broadcast_in_dim.2.skip_ref
  1.8 0.0 copy-done.2
  1.8 0.0 copy-start
  1.8 1.2 copy-done
  3.0 0.0 copy-start.1
  3.0 1.2 copy-done.1
  4.3 0.0 copy-start.3
  4.3 1.0 copy-done.3
  5.3 0.0 copy-start.4
  5.3 1.0 copy-done.4
  6.3 0.0 copy-start.5
  6.3 1.0 copy-done.5
  7.4 159.3 %hyena.1 = bf16[128,2048]{1,0:T(8,128)(2,1)S(1)} custom-call(bf16[128,2048]{1,0:T(8,128)(2,1)S(1)} %copy-done.2, bf16[128,2048]{1,0:T(8,128)(2,1)S(1)} %copy-done.3, bf16[128,2048]{1,0:T(8,128)(2,1)S(1)} %copy-done.4, bf16[128,2048]{1,0:T(8,128)(2,1)S(1)} %copy-done.5, f32[128,1,128]{2,1,0:T(1,128)S(1)} %maximum_convert_fusion.taps_ref, ...), custom_call_target="tpu_custom_call" | custom-call | tf_op jit(solution)/shard_map/hyena/pallas_call | solution.py:400
  166.7 0.8 copy.13
Async XLA Ops:
  0.0 0.8 copy-start.6
  0.0 1.8 %copy-start.2 = (bf16[128,2048]{1,0:T(8,128)(2,1)S(1)}, bf16[128,2048]{1,0:T(8,128)(2,1)}, u32[]{:S(2)}) copy-start(bf16[128,2048]{1,0:T(8,128)(2,1)} %value_ref.1) | copy-start | bytes 1572868
  1.8 1.2 copy-start
  3.0 1.2 copy-start.1
  4.3 1.0 copy-start.3
  5.3 1.0 copy-start.4
  6.3 1.0 copy-start.5
